TPU v7x, 256 devices: a whole 4x4x8 slice. The times are simulated.
256 devices in a mesh: ctx: 128 (over y, z, x), head: 2 (over core).
Axes of the slice: x: 4, y: 4, z: 8, core: 2. Of those that a mesh axis runs over, the one named last changes fastest.
Arguments:
- queries: bfloat16 [2, 49152, 128], P('head', 'ctx'), may hold values from -150 to 150
- keys: bfloat16 [2, 49152, 128], P('head', 'ctx'), may hold values from -8 to 8
- values: bfloat16 [2, 49152, 128], P('head', 'ctx'), may hold values from -6 to 6
- out_weight: bfloat16 [2, 128, 4096], P('head'), may hold values from -0.375 to 0.375
Outputs:
- projected: bfloat16 [49152, 4096], P('ctx', 'head')
All inputs are finite; a program needn't handle non-finite values.
Results may differ from a plain program's by a relative error of at most 0.012.
Values may be sent and summed in bfloat16 or wider, within the bound.
A program may use at most 256 MiB of HBM per device.

v0:
```python
import math

import jax
import jax.numpy as jnp
from jax import lax
from jax.sharding import PartitionSpec as P

big_negative = -1e30


def empty_running(row_count, width):
    return (
        jnp.full((row_count,), big_negative, jnp.float32),
        jnp.zeros((row_count,), jnp.float32),
        jnp.zeros((row_count, width), jnp.float32),
    )


def attend(running, query_rows, query_pos, key_block, value_block, key_pos):
    row_max, row_total, summed = running
    scaling = 1.0 / math.sqrt(query_rows.shape[1])
    scores = (
        lax.dot_general(
            query_rows, key_block, (((1,), (1,)), ((), ())), preferred_element_type=jnp.float32
        )
        * scaling
    )
    scores = jnp.where(key_pos[None, :] <= query_pos[:, None], scores, jnp.float32(big_negative))
    new_max = jnp.maximum(row_max, jnp.max(scores, axis=1))
    exps = jnp.exp(scores - new_max[:, None])
    row_total = jnp.sum(exps, axis=1)
    summed = jnp.dot(exps.astype(jnp.bfloat16), value_block, preferred_element_type=jnp.float32)
    return (new_max, row_total, summed)


def maybe_attend(running, query_rows, query_pos, block_pair, first_row):
    key_pos = jnp.arange(block_pair.shape[1], dtype=jnp.int32)

    def taken(carried):
        return attend(carried, query_rows, query_pos, block_pair[0], block_pair[1], key_pos)

    def skipped(carried):
        return carried

    return lax.cond(first_row <= query_pos[-1], taken, skipped, running)


def finish(running):
    return (running[2] / running[1][:, None]).astype(jnp.bfloat16)


def per_device(queries, keys, values, out_weight):
    my_index = lax.axis_index("ctx")
    row_count = queries.shape[1]
    width = queries.shape[2]
    own_rows = queries[0]
    first_pos = my_index * row_count
    stacked = jnp.stack([keys[0], values[0]])
    query_pos = first_pos + jnp.arange(row_count, dtype=jnp.int32)
    start_state = empty_running(row_count, width)
    folded = maybe_attend(
        start_state,
        own_rows,
        query_pos,
        lax.all_gather(stacked, "ctx", axis=1, tiled=True),
        jnp.int32(0),
    )
    attention = finish(folded)
    partial_out = jnp.dot(attention, out_weight[0], preferred_element_type=jnp.float32)
    return lax.psum_scatter(
        partial_out.astype(jnp.bfloat16), "head", scatter_dimension=1, tiled=True
    )


def solution(mesh):
    placed = (
        P("head", "ctx", None),
        P("head", "ctx", None),
        P("head", "ctx", None),
        P("head", None, None),
    )
    return jax.shard_map(
        per_device, mesh=mesh, in_specs=placed, out_specs=P("ctx", "head"), check_vma=False
    )
```

profile of v0, /device:TPU:24, one launch (start us, length us, event | category | flops | bytes accessed | tf_op | source)
XLA Modules:
  0.0 299.4 jit_solution(8234657178915243321)
XLA Ops:
  6.5 0.0 copy-start
  6.5 0.0 all-gather.2.cloned.1.call-start
  6.5 1.7 pad_maximum_fusion
  8.3 0.0 all-gather.2.cloned.1.call-update
  8.3 0.0 reduce-scatter.2.cloned.1.call-start
  8.4 0.6 slice.9
  9.6 182.9 %all-gather.2.cloned.1.call-done = bf16[2,49152,128]{2,1,0:T(8,128)(2,1)} async-done(((bf16[2,384,128]{2,1,0:T(8,128)(2,1)}), bf16[2,49152,128]{2,1,0:T(8,128)(2,1)}) %all-gather.2.cloned.1.call-update) | async-done | bytes 25165840 | tf_op jit(solution)/shard_map/all_gather | solution.py:65
  192.5 83.9 %conditional.1 = (f32[384]{0:T(512)S(1)}, f32[384,128]{1,0:T(8,128)S(1)}) conditional(s32[]{:T(128)} %bitcast.3, () %tuple.13, (s32[49152]{0:T(1024)S(1)}, s32[384]{0:T(512)S(1)}, bf16[1,384,128]{2,1,0:T(8,128)(2,1)}, bf16[2,49152,128]{2,1,0:T(8,128)(2,1)}) %tuple.14), branch_computations={%region_0.0_spmd, %region_1.4_spmd} | conditional | flops 9814671360 | bytes 252160528 | solution.py:45
  192.5 30.6 %fusion.12 = (f32[384]{0:T(512)S(1)}, f32[384,49152]{1,0:T(8,128)}) fusion(bf16[2,49152,128]{2,1,0:T(8,128)(2,1)} %get-tuple-element.17, bf16[1,384,128]{2,1,0:T(8,128)(2,1)} %get-tuple-element.23, s32[384]{0:T(512)S(1)} %get-tuple-element.15, s32[49152]{0:T(1024)S(1)} %get-tuple-element.14), kind=kOutput, calls=%fused_computation.18 | convolution fusion | flops 4907335168 | bytes 88378368 | tf_op jit(solution)/shard_map/cond/branch_1_fun/dot_general | solution.py:23
  223.2 29.6 %fusion.2 = f32[384,128]{1,0:T(8,128)S(1)} fusion(f32[384,49152]{1,0:T(8,128)} %get-tuple-element.25, f32[384]{0:T(512)S(1)} %broadcast_maximum_fusion, bf16[2,49152,128]{2,1,0:T(8,128)(2,1)} %get-tuple-element.17), kind=kOutput, calls=%fused_computation.4 | convolution fusion | flops 4869586944 | bytes 88278528 | tf_op jit(solution)/shard_map/cond/branch_1_fun/dot_general | solution.py:32
  252.8 23.6 %fusion.1 = f32[384]{0:T(512)S(1)} fusion(f32[384,49152]{1,0:T(8,128)} %get-tuple-element.25, f32[384]{0:T(512)S(1)} %broadcast_maximum_fusion), kind=kLoop, calls=%fused_computation.3 | loop fusion | flops 37748352 | bytes 75500544 | tf_op jit(solution)/shard_map/cond/branch_1_fun/reduce_sum | solution.py:31
  276.4 0.0 copy-done
  276.4 2.7 convolution_convert_fusion
  279.1 0.0 reduce-scatter.2.cloned.1.call-update
  279.1 13.5 %reduce-scatter.2.cloned.1.call-done = bf16[384,2048]{1,0:T(8,128)(2,1)} async-done(((bf16[384,4096]{1,0:T(8,128)(2,1)}), bf16[384,2048]{1,0:T(8,128)(2,1)}) %reduce-scatter.2.cloned.1.call-update) | async-done | bytes 1572880 | tf_op jit(solution)/shard_map/reduce_scatter | solution.py:70
  (3 shorter events, 0.0 us)
Async XLA Ops:
  6.5 269.8 %copy-start = (bf16[1,128,4096]{2,1,0:T(8,128)(2,1)S(1)}, bf16[1,128,4096]{2,1,0:T(8,128)(2,1)}, u32[]{:S(2)}) copy-start(bf16[1,128,4096]{2,1,0:T(8,128)(2,1)} %param.9) | copy-start | bytes 3145732
  6.5 186.0 %all-gather.2.cloned.1.call-start = ((), (), s32[]{:S(2)}) async-start(), calls=%async_computation.1 | async-start | bytes 25362432 | tf_op jit(solution)/shard_map/all_gather | solution.py:65
  8.3 284.3 %reduce-scatter.2.cloned.1.call-start = ((), (), s32[]{:S(2)}) async-start(), calls=%async_computation.2 | async-start | bytes 4718592 | tf_op jit(solution)/shard_map/reduce_scatter | solution.py:70
Sparse Core Ops, SparseCore 0:
  10.9 181.5 all-gather.1
  279.2 13.3 reduce-scatter.1
where the time goes:
time: 301 us; the launch traced here: 299 us
  waiting for transfers between devices  196 us (65%)
  matrix products  62.9 us (21%)
  other arithmetic  25.3 us (8%)
  between operations  14.1 us (5%)
    all_gather x1, waiting for transfers between devices, per_device(): lax.all_gather(stacked, 'ctx', axis=1, tiled=True)  183 us
    dot_general x1, matrix products, attend(): lax.dot_general(query_rows, key_block, (((1,), (1,)), ((), ())), preferre...  30.6 us
    dot_general x1, matrix products, attend(): jnp.dot(exps.astype(jnp.bfloat16), value_block, preferred_element_type=jn...  29.6 us
    reduce_sum x1, other arithmetic, attend(): row_total = jnp.sum(exps, axis=1)  23.6 us
    reduce_scatter x1, waiting for transfers between devices, per_device(): lax.psum_scatter(partial_out.astype(jnp.bfloat16), 'head', scatter_dimens...  13.5 us
  transfers between devices with their start and end apart: 2, of which 2 were waited for; matrix products, arithmetic and copies ran while one was open for 0% of the time, Pallas kernels for 0%

commit v1 on v0

v1 whole, which is shorter than its diff:
```python
import functools
import math

import jax
import jax.numpy as jnp
from jax import lax
from jax.experimental import pallas as pl
from jax.experimental.pallas import tpu as pltpu
from jax.sharding import PartitionSpec as P

MESH = pl.DeviceIdType.MESH
X, Y, Z = 4, 4, 8
ROWS = 384
HALF = ROWS // 2
HD = 128
KEYS = Z * HALF
SUPER = X * ROWS
TILE = 768
BLOCK = 256
SCALE2 = math.log2(math.e) / math.sqrt(HD)
LOW = -1e30
TINY = 1e-30
BF16, F32 = jnp.bfloat16, jnp.float32


def lane_rows(columns):
    parts = [columns[128 * j : 128 * (j + 1), :].T[0:1, :] for j in range(ROWS // 128)]
    return jnp.concatenate(parts, axis=0)


def lane_columns(rows):
    parts = [jnp.broadcast_to(rows[j : j + 1, :], (128, 128)).T for j in range(ROWS // 128)]
    return jnp.concatenate(parts, axis=0)


def pack_stats(rows):
    high = rows.astype(BF16).astype(F32)
    mid = (rows - high).astype(BF16).astype(F32)
    low = rows - high - mid
    return jnp.concatenate([high, mid, low, jnp.zeros((7, 128), F32)], axis=0).astype(BF16)


def unpack_stats(packed):
    wide = packed.astype(F32)
    return wide[0:3] + wide[3:6] + wide[6:9]


def merge(parts):
    top = functools.reduce(jnp.maximum, [stats for _, stats in parts])
    shares = [jnp.exp2(stats - top) for _, stats in parts]
    total = sum(shares)
    merged = None
    for (rows, _), share in zip(parts, shares):
        term = rows.astype(F32) * lane_columns(share / total)
        merged = term if merged is None else merged + term
    return merged, top + jnp.log2(total)


def attention_kernel(
    q_ref, k_ref, v_ref, w_ref, att_ref, w2_ref,
    qbuf, kvbuf, swap, kt, acc, top, obuf, r1, pbuf, r2, att, wx,
    kv_ss, kv_rs, swap_ss, q1_ss, q1_rs, q2_ss, q2_rs, o1_ss, o1_rs, o2_ss, o2_rs, c_ss, c_rs,
):
    index, core = lax.axis_index("ctx"), lax.axis_index("head")
    x, z, y = lax.rem(index, X), lax.rem(lax.div(index, X), Z), lax.div(index, X * Z)

    def at(px, py, pz, pc=None):
        return ((py * Z + pz) * X + px, core if pc is None else pc)

    def ring(p, d, n):
        return lax.rem(p + d + n, n)

    def remote(src, dst, ss, rs, where):
        return pltpu.make_async_remote_copy(
            src_ref=src, dst_ref=dst, send_sem=ss, recv_sem=rs, device_id=where, device_id_type=MESH
        )

    other = 1 - core
    up, down = at(x, y, ring(z, 1, Z)), at(x, y, ring(z, -1, Z))
    partner = at(x, y, z, other)
    x_peers = [at(ring(x, k, X), y, z) for k in range(1, X)]
    y_peers = [at(x, ring(y, k, Y), z) for k in range(1, Y)]
    first = [(jnp.where(core == 0, a[0], b[0]), core) for a, b in zip(x_peers, y_peers)]
    second = [(jnp.where(core == 0, b[0], a[0]), core) for a, b in zip(x_peers, y_peers)]
    u, v = jnp.where(core == 0, y, x), jnp.where(core == 0, x, y)

    barrier = pltpu.get_barrier_semaphore()
    for where in x_peers + y_peers + [up, down, partner]:
        pl.semaphore_signal(barrier, inc=1, device_id=where, device_id_type=MESH)
    pl.semaphore_wait(barrier, 9)

    def slot(h, s):
        return kvbuf.at[h, :, pl.ds(pl.multiple_of(s * HALF, HALF), HALF), :]

    def q_slot(n):
        return qbuf.at[n]

    own = pl.ds(pl.multiple_of(z * HALF, HALF), HALF)
    kvbuf[0, 0, own, :] = k_ref[0:HALF, :]
    kvbuf[0, 1, own, :] = v_ref[0:HALF, :]
    swap[0] = k_ref[HALF:ROWS, :]
    swap[1] = v_ref[HALF:ROWS, :]
    qbuf[u * 4 + v] = q_ref[...]

    mirror = at(x, Y - 1 - y, z)
    swap_copy = remote(swap, slot(1, z), swap_ss, kv_rs.at[1, z], mirror)
    swap_copy.start()

    def ring_copy(h, way, d):
        s = ring(z, -d if way == 0 else d, Z)
        return remote(
            slot(h, s), slot(h, s), kv_ss.at[h, way, d], kv_rs.at[h, s], up if way == 0 else down
        )

    reach = {(0, 0): 4, (0, 1): 3, (1, 0): 3, (1, 1): 4}
    sent = []

    def pass_on(h, way, d):
        if d < reach[h, way]:
            copy = ring_copy(h, way, d)
            copy.start()
            sent.append(copy)

    def arrived(h, way, d):
        if d <= reach[h, way]:
            s = ring(z, -d if way == 0 else d, Z)
            remote(slot(h, s), slot(h, s), kv_ss.at[h, way, 0], kv_rs.at[h, s], up).wait_recv()

    pass_on(0, 0, 0)
    pass_on(0, 1, 0)

    q1 = []
    for k in range(1, 4):
        copy = remote(q_slot(u * 4 + v), q_slot(u * 4 + v), q1_ss.at[k], q1_rs.at[k], first[k - 1])
        copy.start()
        q1.append(copy)
    w_copy = remote(
        w_ref.at[:, pl.ds(pl.multiple_of(other * 2048, 2048), 2048)], wx, c_ss.at[0], c_rs.at[0], partner
    )
    w_copy.start()

    remote(slot(1, z), slot(1, z), swap_ss, kv_rs.at[1, z], mirror).wait_recv()
    pass_on(1, 0, 0)
    pass_on(1, 1, 0)

    for k in range(1, 4):
        s = q_slot(u * 4 + ring(v, -k, 4))
        remote(s, s, q1_ss.at[k], q1_rs.at[k], first[k - 1]).wait_recv()
    q2 = []
    for k in range(1, 4):
        row = qbuf.at[pl.ds(u * 4, 4)]
        copy = remote(row, row, q2_ss.at[k], q2_rs.at[k], second[k - 1])
        copy.start()
        q2.append(copy)

    for d in range(1, 5):
        for h in range(2):
            for way in range(2):
                arrived(h, way, d)
                pass_on(h, way, d)
    for k in range(1, 4):
        row = qbuf.at[pl.ds(ring(u, -k, 4) * 4, 4)]
        remote(row, row, q2_ss.at[k], q2_rs.at[k], second[k - 1]).wait_recv()

    for h in range(2):
        for p in range(4):
            kt[h, :, 384 * p : 384 * (p + 1)] = kvbuf[h, 0, 384 * p : 384 * (p + 1), :].T

    def queries_of(yp, t):
        chunks = []
        for j in range(TILE // ROWS):
            xp = t * (TILE // ROWS) + j
            chunks.append(qbuf[jnp.where(core == 0, yp * 4 + xp, xp * 4 + yp)])
        return jnp.concatenate(chunks, axis=0)

    def step(state, q, keys, values, keep=None):
        old, summed = state
        score = jnp.dot(q, keys, preferred_element_type=F32)
        if keep is not None:
            score = jnp.where(keep, score, LOW)
        new = jnp.maximum(old, jnp.max(score, axis=1, keepdims=True))
        exps = jnp.exp2((score - new) * SCALE2).astype(BF16)
        both = jnp.concatenate([values, jnp.ones((BLOCK, 128), BF16)], axis=1)
        summed = summed * jnp.exp2((old - new) * SCALE2) + jnp.dot(exps, both, preferred_element_type=F32)
        return new, summed

    def load():
        return top[:, 0:1], acc[...]

    def store(state):
        top[...] = jnp.broadcast_to(state[0], (TILE, 128))
        acc[...] = state[1]

    def o1_copy(yp, k):
        xp = ring(x, k, X)
        return remote(obuf.at[yp, xp], r1.at[yp, x], o1_ss.at[yp, k], o1_rs.at[yp, k], at(xp, y, z))

    def o2_copy(yp):
        return remote(pbuf.at[yp], r2.at[y], o2_ss.at[yp], o2_rs.at[y], at(x, yp, z))

    def one_super(yp, _):
        def one_tile(t, _):
            acc[...] = jnp.zeros_like(acc)
            top[...] = jnp.full_like(top, LOW)
            q = queries_of(yp, t)

            def one_group(h, _):
                ky = jnp.where(h == 0, y, Y - 1 - y)

                @pl.when(yp > ky)
                def _():
                    state = load()
                    for b in range(KEYS // BLOCK):
                        span = slice(b * BLOCK, (b + 1) * BLOCK)
                        state = step(state, q, kt[h, :, span], kvbuf[h, 1, span, :])
                    store(state)

                @pl.when(yp == ky)
                def _():
                    count = lax.div(HALF * z + HALF - 1, BLOCK) + 1
                    query = t * TILE + z * SUPER + lax.broadcasted_iota(jnp.int32, (TILE, BLOCK), 0)

                    def masked(b, _):
                        span = pl.ds(pl.multiple_of(b * BLOCK, BLOCK), BLOCK)
                        n = b * BLOCK + lax.broadcasted_iota(jnp.int32, (1, BLOCK), 1)
                        place = n + (x * ROWS + h * HALF)
                        for edge in range(1, Z):
                            place = place + jnp.where(n >= edge * HALF, SUPER - HALF, 0)
                        store(step(load(), q, kt[h, :, span], kvbuf[h, 1, span, :], place <= query))
                        return 0

                    lax.fori_loop(0, count, masked, 0)

                return 0

            lax.fori_loop(0, 2, one_group, 0)
            for j in range(TILE // ROWS):
                span = slice(j * ROWS, (j + 1) * ROWS)
                total = jnp.maximum(acc[span, 128:256], TINY)
                xp = t * (TILE // ROWS) + j
                obuf[yp, xp, 0:ROWS, :] = (acc[span, 0:128] / total).astype(BF16)
                stats = top[span, :] * SCALE2 + jnp.log2(total)
                obuf[yp, xp, ROWS : ROWS + 16, :] = pack_stats(lane_rows(stats))
            return 0

        lax.fori_loop(0, SUPER // TILE, one_tile, 0)
        for k in range(1, 4):
            o1_copy(yp, k).start()
        r1[yp, x] = obuf[yp, x]
        return 0

    lax.fori_loop(0, Y, one_super, 0)

    def read(ref):
        return ref[0:ROWS, :], unpack_stats(ref[ROWS : ROWS + 16, :])

    def first_merge(yp, _):
        for k in range(1, 4):
            s = r1.at[yp, ring(x, -k, X)]
            remote(s, s, o1_ss.at[yp, k], o1_rs.at[yp, k], partner).wait_recv()
        merged, stats = merge([read(r1.at[yp, s]) for s in range(4)])
        pbuf[yp, 0:ROWS, :] = merged.astype(BF16)
        pbuf[yp, ROWS : ROWS + 16, :] = pack_stats(stats)

        @pl.when(yp != y)
        def _():
            o2_copy(yp).start()

        @pl.when(yp == y)
        def _():
            r2[y] = pbuf[yp]

        return 0

    lax.fori_loop(0, Y, first_merge, 0)

    for k in range(1, 4):
        s = ring(y, k, Y)
        remote(r2.at[s], r2.at[s], o2_ss.at[0], o2_rs.at[s], partner).wait_recv()
    merged, _ = merge([read(r2.at[s]) for s in range(4)])
    att[core] = merged.astype(BF16)
    att_copy = remote(att.at[core], att.at[core], c_ss.at[1], c_rs.at[1], partner)
    att_copy.start()

    swap_copy.wait_send()
    for copy in sent + q1 + q2:
        copy.wait_send()

    def drain(yp, _):
        for k in range(1, 4):
            o1_copy(yp, k).wait_send()

        @pl.when(yp != y)
        def _():
            o2_copy(yp).wait_send()

        return 0

    lax.fori_loop(0, Y, drain, 0)
    w_copy.wait()
    w2_ref[core] = w_ref[:, pl.ds(pl.multiple_of(core * 2048, 2048), 2048)]
    w2_ref[other] = wx[...]
    att_copy.wait_send()
    remote(att.at[other], att.at[other], c_ss.at[1], c_rs.at[1], partner).wait_recv()
    att_ref[...] = att[...]


def project_kernel(att_ref, w_ref, out_ref):
    out_ref[...] = (
        jnp.dot(att_ref[0], w_ref[0], preferred_element_type=F32)
        + jnp.dot(att_ref[1], w_ref[1], preferred_element_type=F32)
    ).astype(BF16)


def per_device(queries, keys, values, out_weight):
    vmem = pl.BlockSpec(memory_space=pltpu.VMEM)
    dma = pltpu.SemaphoreType.DMA
    att, w2 = pl.pallas_call(
        attention_kernel,
        out_shape=(
            jax.ShapeDtypeStruct((2, ROWS, HD), BF16),
            jax.ShapeDtypeStruct((2, HD, 2048), BF16),
        ),
        in_specs=[vmem] * 4,
        out_specs=(vmem, vmem),
        scratch_shapes=[
            pltpu.VMEM((16, ROWS, HD), BF16),
            pltpu.VMEM((2, 2, KEYS, HD), BF16),
            pltpu.VMEM((2, HALF, HD), BF16),
            pltpu.VMEM((2, HD, KEYS), BF16),
            pltpu.VMEM((TILE, 256), F32),
            pltpu.VMEM((TILE, 128), F32),
            pltpu.VMEM((4, 4, ROWS + 16, HD), BF16),
            pltpu.VMEM((4, 4, ROWS + 16, HD), BF16),
            pltpu.VMEM((4, ROWS + 16, HD), BF16),
            pltpu.VMEM((4, ROWS + 16, HD), BF16),
            pltpu.VMEM((2, ROWS, HD), BF16),
            pltpu.VMEM((HD, 2048), BF16),
            dma((2, 2, 4)), dma((2, 8)), dma, dma((4,)), dma((4,)), dma((4,)), dma((4,)),
            dma((4, 4)), dma((4, 4)), dma((4,)), dma((4,)), dma((2,)), dma((2,)),
        ],
        compiler_params=pltpu.CompilerParams(
            collective_id=0, has_side_effects=True, vmem_limit_bytes=50 << 20
        ),
    )(queries[0], keys[0], values[0], out_weight[0])
    return pl.pallas_call(
        project_kernel,
        grid=(4,),
        out_shape=jax.ShapeDtypeStruct((ROWS, 2048), BF16),
        in_specs=[
            pl.BlockSpec((2, ROWS, HD), lambda n: (0, 0, 0)),
            pl.BlockSpec((2, HD, 512), lambda n: (0, 0, n)),
        ],
        out_specs=pl.BlockSpec((ROWS, 512), lambda n: (0, n)),
    )(att, w2)


def solution(mesh):
    placed = (
        P("head", "ctx", None),
        P("head", "ctx", None),
        P("head", "ctx", None),
        P("head", None, None),
    )
    return jax.shard_map(
        per_device, mesh=mesh, in_specs=placed, out_specs=P("ctx", "head"), check_vma=False
    )
```

time: 301 us -> 110 us (0.37)
  the two profiles are of different devices: /device:TPU:24 before, /device:TPU:217 now
where the time goes in v1:
time: 110 us
  Pallas kernels  104 us (95%)
  local copies, waits for them, and re-layouts  5.54 us (5%)
    pallas_call x1, Pallas kernels, per_device(): pl.pallas_call(attention_kernel, out_shape=(jax.ShapeDtypeStruct((2, ROWS...  100 us
    unnamed x12, local copies, waits for them, and re-layouts  5.54 us
    pallas_call x1, Pallas kernels, per_device(): pl.pallas_call(project_kernel, grid=(4,), out_shape=jax.ShapeDtypeStruct(...  4.16 us

profile of v1, /device:TPU:217, one launch (start us, length us, event | category | flops | bytes accessed | tf_op | source)
XLA Modules:
  0.0 110.0 jit_solution(7203171850719355107)
XLA Ops:
  0.0 0.0 copy-start
  0.0 1.2 %copy-done = bf16[1,128,4096]{2,1,0:T(8,128)(2,1)S(1)} copy-done((bf16[1,128,4096]{2,1,0:T(8,128)(2,1)S(1)}, bf16[1,128,4096]{2,1,0:T(8,128)(2,1)}, u32[]{:S(2)}) %copy-start) | copy-done | bytes 1048600
  1.2 0.0 copy-start.3
  1.2 0.9 copy-done.3
  2.1 0.0 copy-start.4
  2.1 0.9 copy-done.4
  3.0 0.0 copy-start.5
  3.0 0.9 copy-done.5
  3.9 100.3 %shard_map.46 = (bf16[2,384,128]{2,1,0:T(8,128)(2,1)S(1)}, bf16[2,128,2048]{2,1,0:T(8,128)(2,1)S(1)}) custom-call(bf16[384,128]{1,0:T(8,128)(2,1)S(1)} %bitcast.5, bf16[384,128]{1,0:T(8,128)(2,1)S(1)} %bitcast.6, bf16[384,128]{1,0:T(8,128)(2,1)S(1)} %bitcast.7, bf16[128,4096]{1,0:T(8,128)(2,1)S(1)} %bitcast.4), custom_call_target="tpu_custom_call" | custom-call | tf_op jit(solution)/shard_map/pallas_call | solution.py:318
  104.2 0.0 copy-start.1
  104.2 1.0 copy-done.1
  105.2 0.0 copy-start.2
  105.2 0.7 copy-done.2
  105.8 4.2 %shard_map.47 = bf16[384,2048]{1,0:T(8,128)(2,1)} custom-call(bf16[2,384,128]{2,1,0:T(8,128)(2,1)} %copy-done.2, bf16[2,128,2048]{2,1,0:T(8,128)(2,1)} %copy-done.1), custom_call_target="tpu_custom_call" | custom-call | tf_op jit(solution)/shard_map/pallas_call | solution.py:346
Async XLA Ops:
  0.0 1.2 %copy-start = (bf16[1,128,4096]{2,1,0:T(8,128)(2,1)S(1)}, bf16[1,128,4096]{2,1,0:T(8,128)(2,1)}, u32[]{:S(2)}) copy-start(bf16[1,128,4096]{2,1,0:T(8,128)(2,1)} %param.7) | copy-start | bytes 3145732
  1.2 0.9 copy-start.3
  2.1 0.9 copy-start.4
  3.0 0.9 copy-start.5
  104.2 1.0 copy-start.1
  105.2 0.7 copy-start.2

commit v2 on v0

v2 whole, which is shorter than its diff:
```python
import functools
import math

import jax
import jax.numpy as jnp
from jax import lax
from jax.experimental import pallas as pl
from jax.experimental.pallas import tpu as pltpu
from jax.sharding import PartitionSpec as P

MESH = pl.DeviceIdType.MESH
X, Y, Z = 4, 4, 8
ROWS = 384
HALF = ROWS // 2
HD = 128
LINE = Z * HALF
SUPER = X * ROWS
TILE = LINE // 2
BLOCK = 256
WIDTH = 2048
MESSAGE = HALF + 16
SCALE2 = math.log2(math.e) / math.sqrt(HD)
LOW = -1e30
TINY = 1e-30
BF16, F32 = jnp.bfloat16, jnp.float32


def lane_rows(columns):
    return jnp.concatenate([columns[0:128].T[0:1], columns[HALF - 128 : HALF].T[0:1]], axis=0)


def lane_columns(rows):
    low = jnp.broadcast_to(rows[0:1], (128, 128)).T
    high = jnp.broadcast_to(rows[1:2], (128, 128)).T
    return jnp.concatenate([low, high[256 - HALF : 128]], axis=0)


def pack_stats(rows):
    high = rows.astype(BF16).astype(F32)
    mid = (rows - high).astype(BF16).astype(F32)
    low = rows - high - mid
    return jnp.concatenate([high, mid, low, jnp.zeros((10, 128), F32)], axis=0).astype(BF16)


def unpack_stats(packed):
    wide = packed.astype(F32)
    return wide[0:2] + wide[2:4] + wide[4:6]


def attention_kernel(
    q_ref, k_ref, v_ref, w_ref, out_ref,
    qbuf, kvbuf, kt, swap, acc, top, obuf, rbuf, att, w2, proj,
    in_s, kv1_ss, kv2_ss, kv_rs, swap_ss, q_ss, q_rs, o_ss, o_rs, c_ss, c_rs, out_s,
):
    index, core = lax.axis_index("ctx"), lax.axis_index("head")
    x, z, y = lax.rem(index, X), lax.rem(lax.div(index, X), Z), lax.div(index, X * Z)
    ym = Y - 1 - y

    def at(px, py, pz, pc=None):
        return ((py * Z + pz) * X + px, core if pc is None else pc)

    def ring(p, d, n):
        return lax.rem(p + d + n, n)

    def remote(src, dst, ss, rs, where):
        return pltpu.make_async_remote_copy(
            src_ref=src, dst_ref=dst, send_sem=ss, recv_sem=rs, device_id=where, device_id_type=MESH
        )

    other = 1 - core
    partner = at(x, y, z, other)
    x_peers = [at(ring(x, k, X), y, z) for k in range(1, X)]
    y_peers = [at(x, ring(y, k, Y), z) for k in range(1, Y)]
    lines = [[at(x, yy, ring(z, k, Z)) for k in range(Z)] for yy in (y, ym)]
    first = [(jnp.where(core == 0, a[0], b[0]), core) for a, b in zip(x_peers, y_peers)]
    second = [(jnp.where(core == 0, b[0], a[0]), core) for a, b in zip(x_peers, y_peers)]

    def rows_at(n, size):
        return pl.ds(pl.multiple_of(n * size, size), size)

    def chunk(n):
        return kvbuf.at[:, rows_at(n, ROWS), :]

    mine = y * X + x
    loads = [
        pltpu.make_async_copy(k_ref, kvbuf.at[0, rows_at(mine, ROWS)], in_s.at[0]),
        pltpu.make_async_copy(v_ref, kvbuf.at[1, rows_at(mine, ROWS)], in_s.at[1]),
        pltpu.make_async_copy(q_ref.at[0:HALF], qbuf.at[0, rows_at(z, HALF)], in_s.at[2]),
        pltpu.make_async_copy(q_ref.at[HALF:ROWS], swap, in_s.at[3]),
        pltpu.make_async_copy(
            w_ref.at[:, rows_at(core, WIDTH)], w2.at[rows_at(core, HD)], in_s.at[4]
        ),
    ]
    for copy in loads:
        copy.start()

    barrier = pltpu.get_barrier_semaphore()
    for where in lines[0][1:] + lines[1] + x_peers + y_peers + [partner]:
        pl.semaphore_signal(barrier, inc=1, device_id=where, device_id_type=MESH)
    pl.semaphore_wait(barrier, 22)

    sent = []

    def send(copy):
        copy.start()
        sent.append(copy)

    for copy in loads[:4]:
        copy.wait()
    for k in (1, 3, 2):
        send(remote(chunk(mine), chunk(mine), kv1_ss.at[k], kv_rs.at[mine], first[k - 1]))
    own_rows = [qbuf.at[h, rows_at(z, HALF)] for h in range(2)]
    send(remote(swap, own_rows[1], swap_ss, q_rs.at[1, z], lines[1][0]))
    for k in (1, 7, 2, 6, 3, 5, 4):
        send(remote(own_rows[0], own_rows[0], q_ss.at[0, k], q_rs.at[0, z], lines[0][k]))
    for k in (1, 3, 2):
        send(remote(chunk(mine), chunk(mine), kv2_ss.at[0, k], kv_rs.at[mine], second[k - 1]))
    remote(own_rows[1], own_rows[1], swap_ss, q_rs.at[1, z], partner).wait_recv()
    for k in (1, 7, 2, 6, 3, 5, 4):
        send(remote(own_rows[1], own_rows[1], q_ss.at[1, k], q_rs.at[1, z], lines[0][k]))
    send(
        remote(
            w_ref.at[:, rows_at(other, WIDTH)], w2.at[rows_at(core, HD)], c_ss.at[0], c_rs.at[0], partner
        )
    )

    def clear(n, _):
        acc[n] = jnp.zeros((LINE, 256), F32)
        top[n] = jnp.full((LINE, 128), LOW, F32)
        return 0

    lax.fori_loop(0, 2, clear, 0)

    for j in (1, 3, 2):
        n = jnp.where(core == 0, y * X + ring(x, -j, X), ring(y, -j, Y) * X + x)
        remote(chunk(n), chunk(n), kv1_ss.at[j], kv_rs.at[n], partner).wait_recv()
        for k in (1, 3, 2):
            send(remote(chunk(n), chunk(n), kv2_ss.at[j, k], kv_rs.at[n], second[k - 1]))

    def step(state, q, keys, values, keep=None):
        old, summed = state
        score = jnp.dot(q, keys, preferred_element_type=F32)
        if keep is not None:
            score = jnp.where(keep, score, LOW)
        new = jnp.maximum(old, jnp.max(score, axis=1, keepdims=True))
        exps = jnp.exp2((score - new) * SCALE2).astype(BF16)
        both = jnp.concatenate([values, jnp.ones(values.shape, BF16)], axis=1)
        summed = summed * jnp.exp2((old - new) * SCALE2) + jnp.dot(exps, both, preferred_element_type=F32)
        return new, summed

    def attend(h, start, count, yp, limit=None):
        span = pl.ds(pl.multiple_of(start, count), count)
        q = qbuf[h, span, :]
        state = top[h, span, 0:1], acc[h, span, :]
        for b in range(SUPER // BLOCK):
            values = kvbuf[1, pl.ds(pl.multiple_of(yp * SUPER + b * BLOCK, BLOCK), BLOCK), :]
            keep = None
            if limit is not None:
                keep = b * BLOCK + lax.broadcasted_iota(jnp.int32, (count, BLOCK), 1) <= limit
            state = step(state, q, kt[yp, :, b * BLOCK : (b + 1) * BLOCK], values, keep)
        top[h, span, :] = jnp.broadcast_to(state[0], (count, 128))
        acc[h, span, :] = state[1]

    def task(h, g, yp):
        yq = jnp.where(h == 0, y, ym)

        @pl.when(yp < yq)
        def _():
            attend(h, g * TILE, TILE, yp)

        @pl.when(yp == yq)
        def _():
            edge = lax.div(z, 2)

            def pair(i, _):
                @pl.when(i > edge)
                def _():
                    attend(h, i * ROWS, ROWS, yp)

                @pl.when(i == edge)
                def _():
                    row = lax.broadcasted_iota(jnp.int32, (ROWS, 1), 0)
                    here = row + (x * ROWS + h * HALF)
                    low = jnp.where(lax.rem(z, 2) == 0, here, -1)
                    high = jnp.where(lax.rem(z, 2) == 0, SUPER, here - HALF)
                    attend(h, i * ROWS, ROWS, yp, jnp.where(row < HALF, low, high))

                return 0

            lax.fori_loop(2 * g, 2 * g + 2, pair, 0)

    def need_keys(yp):
        for xp in range(X):
            n = yp * X + xp

            @pl.when(jnp.where(core == 0, yp != y, x != xp))
            def _():
                remote(chunk(n), chunk(n), kv1_ss.at[0], kv_rs.at[n], partner).wait_recv()

        for p in range(4):
            rows = pl.ds(pl.multiple_of(yp * SUPER + ROWS * p, ROWS), ROWS)
            kt[yp, :, ROWS * p : ROWS * (p + 1)] = kvbuf[0, rows, :].T

    def need_queries(h, g):
        for t in range(4):
            s = 4 * g + t

            @pl.when(s != z)
            def _():
                r = qbuf.at[h, rows_at(s, HALF)]
                remote(r, r, q_ss.at[0, 0], q_rs.at[h, s], partner).wait_recv()

    def o_copy(h, s):
        where = at(x, jnp.where(h == 0, y, ym), s)
        return remote(obuf.at[h, s], rbuf.at[h, z], o_ss.at[h, s], o_rs.at[h, z], where)

    def finish(h, g):
        def one(t, _):
            s = 4 * g + t
            span = rows_at(s, HALF)
            total = jnp.maximum(acc[h, span, 128:256], TINY)
            obuf[h, s, 0:HALF, :] = (acc[h, span, 0:128] / total).astype(BF16)
            stats = top[h, span, :] * SCALE2 + jnp.log2(total)
            obuf[h, s, HALF:MESSAGE, :] = pack_stats(lane_rows(stats))

            @pl.when((h == 1) | (s != z))
            def _():
                o_copy(h, s).start()

            @pl.when((h == 0) & (s == z))
            def _():
                rbuf[0, z] = obuf[0, z]

            return 0

        lax.fori_loop(0, 4, one, 0)

    def superblock(e):
        return ring(y, jnp.where(e == 0, 0, jnp.where(e == 1, 3, e - 1)), Y)

    near = lax.div(z, 4)

    def work(i, _):
        early = i < 8
        late = i - 8
        e = jnp.where(early, lax.div(i, 4), 2 + lax.rem(i, 2))
        j = jnp.where(early, 3 - lax.rem(i, 4), lax.div(late, 2))
        h = 1 - lax.div(j, 2)
        g = jnp.where(lax.rem(j, 2) == 0, 1 - near, near)
        yp = superblock(e)

        @pl.when((early & (lax.rem(i, 4) == 0)) | (i == 8) | (i == 9))
        def _():
            need_keys(yp)

        @pl.when(i < 4)
        def _():
            need_queries(h, g)

        task(h, g, yp)

        @pl.when((i > 8) & (lax.rem(i, 2) == 1))
        def _():
            finish(h, g)

        return 0

    lax.fori_loop(0, 16, work, 0)

    def merge(h, _):
        for s in range(Z):

            @pl.when((h == 1) | (z != s))
            def _():
                remote(rbuf.at[h, s], rbuf.at[h, s], o_ss.at[0, 0], o_rs.at[h, s], partner).wait_recv()

        stats = [unpack_stats(rbuf[h, s, HALF:MESSAGE, :]) for s in range(Z)]
        highest = functools.reduce(jnp.maximum, stats)
        shares = [jnp.exp2(one - highest) for one in stats]
        total = functools.reduce(jnp.add, shares)
        merged = jnp.zeros((HALF, HD), F32)
        for s in range(Z):
            merged = merged + rbuf[h, s, 0:HALF, :].astype(F32) * lane_columns(shares[s] / total)
        att[core, rows_at(h, HALF), :] = merged.astype(BF16)
        return 0

    lax.fori_loop(0, 2, merge, 0)
    att_copy = remote(att.at[core], att.at[core], c_ss.at[1], c_rs.at[1], partner)
    att_copy.start()

    for copy in sent:
        copy.wait_send()

    def drain(s, _):
        for h in range(2):

            @pl.when((h == 1) | (s != z))
            def _():
                o_copy(h, s).wait_send()

        return 0

    lax.fori_loop(0, Z, drain, 0)
    loads[4].wait()
    w_other = w2.at[rows_at(other, HD)]
    remote(w_other, w_other, c_ss.at[0], c_rs.at[0], partner).wait_recv()
    att_copy.wait_send()
    remote(att.at[other], att.at[other], c_ss.at[1], c_rs.at[1], partner).wait_recv()
    both = jnp.concatenate([att[0], att[1]], axis=1)
    outs = []
    for n in range(4):
        span = slice(n * 512, (n + 1) * 512)
        proj[:, span] = jnp.dot(both, w2[:, span], preferred_element_type=F32).astype(BF16)
        copy = pltpu.make_async_copy(proj.at[:, span], out_ref.at[:, span], out_s.at[n])
        copy.start()
        outs.append(copy)
    for copy in outs:
        copy.wait()


def per_device(queries, keys, values, out_weight):
    hbm = pl.BlockSpec(memory_space=pl.ANY)
    dma = pltpu.SemaphoreType.DMA
    return pl.pallas_call(
        attention_kernel,
        out_shape=jax.ShapeDtypeStruct((ROWS, WIDTH), BF16),
        in_specs=[hbm] * 4,
        out_specs=hbm,
        scratch_shapes=[
            pltpu.VMEM((2, LINE, HD), BF16),
            pltpu.VMEM((2, Y * SUPER, HD), BF16),
            pltpu.VMEM((Y, HD, SUPER), BF16),
            pltpu.VMEM((HALF, HD), BF16),
            pltpu.VMEM((2, LINE, 256), F32),
            pltpu.VMEM((2, LINE, 128), F32),
            pltpu.VMEM((2, Z, MESSAGE, HD), BF16),
            pltpu.VMEM((2, Z, MESSAGE, HD), BF16),
            pltpu.VMEM((2, ROWS, HD), BF16),
            pltpu.VMEM((2 * HD, WIDTH), BF16),
            pltpu.VMEM((ROWS, WIDTH), BF16),
            dma((5,)), dma((4,)), dma((4, 4)), dma((16,)), dma, dma((2, 8)), dma((2, 8)), dma((2, 8)), dma((2, 8)),
            dma((2,)), dma((2,)), dma((4,)),
        ],
        compiler_params=pltpu.CompilerParams(
            collective_id=0, has_side_effects=True, vmem_limit_bytes=56 << 20
        ),
    )(queries[0], keys[0], values[0], out_weight[0])


def solution(mesh):
    placed = (
        P("head", "ctx", None),
        P("head", "ctx", None),
        P("head", "ctx", None),
        P("head", None, None),
    )
    return jax.shard_map(
        per_device, mesh=mesh, in_specs=placed, out_specs=P("ctx", "head"), check_vma=False
    )
```

time: 301 us -> 89.1 us (0.30)
  the two profiles are of different devices: /device:TPU:24 before, /device:TPU:1 now
where the time goes in v2:
time: 89.1 us; the launch traced here: 89 us
  Pallas kernels  86.2 us (97%)
  local copies, waits for them, and re-layouts  2.73 us (3%)
    pallas_call x1, Pallas kernels, per_device(): pl.pallas_call(attention_kernel, out_shape=jax.ShapeDtypeStruct((ROWS, WI...  86.2 us
    unnamed x1, local copies, waits for them, and re-layouts  2.73 us

profile of v2, /device:TPU:1, one launch (start us, length us, event | category | flops | bytes accessed | tf_op | source)
XLA Modules:
  0.0 89.0 jit_solution(16658141209514416958)
XLA Ops:
  0.0 86.2 %shard_map.46 = bf16[384,2048]{1,0:T(8,128)(2,1)} custom-call(bf16[384,128]{1,0:T(8,128)(2,1)} %bitcast.5, bf16[384,128]{1,0:T(8,128)(2,1)} %bitcast.6, bf16[384,128]{1,0:T(8,128)(2,1)} %bitcast.7, bf16[128,4096]{1,0:T(8,128)(2,1)} %bitcast.4), custom_call_target="tpu_custom_call" | custom-call | tf_op jit(solution)/shard_map/pallas_call | solution.py:324
  86.3 2.7 %copy.6 = bf16[384,2048]{1,0:T(8,128)(2,1)} copy(bf16[384,2048]{1,0:T(8,128)(2,1)} %shard_map.46) | data formatting | bytes 3145728

commit v3 on v2

--- a/solution.py
+++ b/solution.py
@@ -16,7 +16,7 @@
 LINE = Z * HALF
 SUPER = X * ROWS
 TILE = LINE // 2
-BLOCK = 256
+BLOCK = 512
 WIDTH = 2048
 MESSAGE = HALF + 16
 SCALE2 = math.log2(math.e) / math.sqrt(HD)
@@ -55,6 +55,7 @@
     index, core = lax.axis_index("ctx"), lax.axis_index("head")
     x, z, y = lax.rem(index, X), lax.rem(lax.div(index, X), Z), lax.div(index, X * Z)
     ym = Y - 1 - y
+    near = lax.div(z, 4)
 
     def at(px, py, pz, pc=None):
         return ((py * Z + pz) * X + px, core if pc is None else pc)
@@ -137,57 +138,86 @@
         for k in (1, 3, 2):
             send(remote(chunk(n), chunk(n), kv2_ss.at[j, k], kv_rs.at[n], second[k - 1]))
 
-    def step(state, q, keys, values, keep=None):
-        old, summed = state
-        score = jnp.dot(q, keys, preferred_element_type=F32)
-        if keep is not None:
-            score = jnp.where(keep, score, LOW)
-        new = jnp.maximum(old, jnp.max(score, axis=1, keepdims=True))
-        exps = jnp.exp2((score - new) * SCALE2).astype(BF16)
-        both = jnp.concatenate([values, jnp.ones(values.shape, BF16)], axis=1)
-        summed = summed * jnp.exp2((old - new) * SCALE2) + jnp.dot(exps, both, preferred_element_type=F32)
-        return new, summed
-
-    def attend(h, start, count, yp, limit=None):
-        span = pl.ds(pl.multiple_of(start, count), count)
-        q = qbuf[h, span, :]
-        state = top[h, span, 0:1], acc[h, span, :]
+    def spread(parts):
+        highest = jnp.max(functools.reduce(jnp.maximum, parts), axis=1, keepdims=True)
+        return jnp.broadcast_to(highest, parts[0].shape)
+
+    def twice(a):
+        return jnp.concatenate([a, a], axis=1)
+
+    def weigh(pieces, new):
+        return jnp.concatenate([jnp.exp2((one - new) * SCALE2).astype(BF16) for one in pieces], axis=1)
+
+    def score(h, span, yp, b):
+        keys = kt[yp, :, b * BLOCK : (b + 1) * BLOCK]
+        both = jnp.dot(qbuf[h, span, :], keys, preferred_element_type=F32)
+        return [both[:, n * 128 : (n + 1) * 128] for n in range(BLOCK // 128)]
+
+    def values_of(yp, start, count):
+        values = kvbuf[1, pl.ds(pl.multiple_of(yp * SUPER + start, BLOCK), count), :]
+        return jnp.concatenate([values, jnp.ones(values.shape, BF16)], axis=1)
+
+    def attend(h, g, yp):
+        spans = [pl.ds(pl.multiple_of(g * TILE + t * ROWS, ROWS), ROWS) for t in range(TILE // ROWS)]
+
+        def scores(span):
+            return [piece for b in range(SUPER // BLOCK) for piece in score(h, span, yp, b)]
+
+        pieces = scores(spans[0])
+        for t, span in enumerate(spans):
+            later = scores(spans[t + 1]) if t + 1 < len(spans) else None
+            old = top[h, span, :]
+            new = jnp.maximum(old, spread(pieces))
+            added = jnp.dot(weigh(pieces, new), values_of(yp, 0, SUPER), preferred_element_type=F32)
+            acc[h, span, :] = acc[h, span, :] * twice(jnp.exp2((old - new) * SCALE2)) + added
+            top[h, span, :] = new
+            pieces = later
+
+    def attend_below(h, i, yp, limit):
+        span = pl.ds(pl.multiple_of(i * ROWS, ROWS), ROWS)
+        lane = lax.broadcasted_iota(jnp.int32, (ROWS, 128), 1)
+
+        def kept(b):
+            pieces = score(h, span, yp, b)
+            return [
+                jnp.where(lane + (b * BLOCK + n * 128) <= limit, one, LOW) for n, one in enumerate(pieces)
+            ]
+
+        old, summed = top[h, span, :], acc[h, span, :]
+        pieces = kept(0)
         for b in range(SUPER // BLOCK):
-            values = kvbuf[1, pl.ds(pl.multiple_of(yp * SUPER + b * BLOCK, BLOCK), BLOCK), :]
-            keep = None
-            if limit is not None:
-                keep = b * BLOCK + lax.broadcasted_iota(jnp.int32, (count, BLOCK), 1) <= limit
-            state = step(state, q, kt[yp, :, b * BLOCK : (b + 1) * BLOCK], values, keep)
-        top[h, span, :] = jnp.broadcast_to(state[0], (count, 128))
-        acc[h, span, :] = state[1]
+            later = kept(b + 1) if b + 1 < SUPER // BLOCK else None
+            new = jnp.maximum(old, spread(pieces))
+            added = jnp.dot(
+                weigh(pieces, new), values_of(yp, b * BLOCK, BLOCK), preferred_element_type=F32
+            )
+            summed = summed * twice(jnp.exp2((old - new) * SCALE2)) + added
+            old, pieces = new, later
+        top[h, span, :] = old
+        acc[h, span, :] = summed
 
     def task(h, g, yp):
         yq = jnp.where(h == 0, y, ym)
 
-        @pl.when(yp < yq)
-        def _():
-            attend(h, g * TILE, TILE, yp)
-
-        @pl.when(yp == yq)
+        @pl.when((yp < yq) | ((yp == yq) & (g > near)))
+        def _():
+            attend(h, g, yp)
+
+        @pl.when((yp == yq) & (g == near))
         def _():
             edge = lax.div(z, 2)
 
             def pair(i, _):
-                @pl.when(i > edge)
-                def _():
-                    attend(h, i * ROWS, ROWS, yp)
-
-                @pl.when(i == edge)
-                def _():
-                    row = lax.broadcasted_iota(jnp.int32, (ROWS, 1), 0)
-                    here = row + (x * ROWS + h * HALF)
-                    low = jnp.where(lax.rem(z, 2) == 0, here, -1)
-                    high = jnp.where(lax.rem(z, 2) == 0, SUPER, here - HALF)
-                    attend(h, i * ROWS, ROWS, yp, jnp.where(row < HALF, low, high))
-
+                row = lax.broadcasted_iota(jnp.int32, (ROWS, 128), 0)
+                here = row + (x * ROWS + h * HALF)
+                even = lax.rem(z, 2) == 0
+                low = jnp.where(even, here, -1)
+                high = jnp.where(even, SUPER, here - HALF)
+                limit = jnp.where(row < HALF, low, high)
+                attend_below(h, i, yp, jnp.where(i > edge, SUPER, limit))
                 return 0
 
-            lax.fori_loop(2 * g, 2 * g + 2, pair, 0)
+            lax.fori_loop(edge, 2 * g + 2, pair, 0)
 
     def need_keys(yp):
         for xp in range(X):
@@ -237,8 +267,6 @@
 
     def superblock(e):
         return ring(y, jnp.where(e == 0, 0, jnp.where(e == 1, 3, e - 1)), Y)
-
-    near = lax.div(z, 4)
 
     def work(i, _):
         early = i < 8

time: 89.1 us -> 65.6 us (0.74)
  Pallas kernels: 86.2 us -> 62.8 us
    pallas_call x1, Pallas kernels: 86.2 us -> 62.8 us  [per_device(): pl.pallas_call(attention_kernel, out_shape=jax.ShapeDtypeStruct((ROWS, WI...]
where the time goes in v3:
time: 65.6 us; the launch traced here: 65.5 us
  Pallas kernels  62.8 us (96%)
  local copies, waits for them, and re-layouts  2.73 us (4%)
    pallas_call x1, Pallas kernels, per_device(): pl.pallas_call(attention_kernel, out_shape=jax.ShapeDtypeStruct((ROWS, WI...  62.8 us
    unnamed x1, local copies, waits for them, and re-layouts  2.73 us

profile of v3, /device:TPU:1, one launch (start us, length us, event | category | flops | bytes accessed | tf_op | source)
XLA Modules:
  0.0 65.5 jit_solution(13071776986890095154)
XLA Ops:
  0.0 62.8 %shard_map.46 = bf16[384,2048]{1,0:T(8,128)(2,1)} custom-call(bf16[384,128]{1,0:T(8,128)(2,1)} %bitcast.5, bf16[384,128]{1,0:T(8,128)(2,1)} %bitcast.6, bf16[384,128]{1,0:T(8,128)(2,1)} %bitcast.7, bf16[128,4096]{1,0:T(8,128)(2,1)} %bitcast.4), custom_call_target="tpu_custom_call" | custom-call | tf_op jit(solution)/shard_map/pallas_call | solution.py:352
  62.8 2.7 %copy.6 = bf16[384,2048]{1,0:T(8,128)(2,1)} copy(bf16[384,2048]{1,0:T(8,128)(2,1)} %shard_map.46) | data formatting | bytes 3145728

commit v4 on v3

--- a/solution.py
+++ b/solution.py
@@ -102,20 +102,33 @@
 
     sent = []
 
-    def send(copy):
-        copy.start()
-        sent.append(copy)
+    def when(condition, act):
+        if condition is None:
+            act()
+        else:
+            pl.when(condition)(act)
+
+    def send(copy, condition=None):
+        when(condition, copy.start)
+        sent.append((condition, copy))
+
+    def needed(source, target):
+        return (source <= target) | (source <= Y - 1 - target)
+
+    y_targets = [needed(y, ring(y, k, Y)) for k in range(1, Y)]
 
     for copy in loads[:4]:
         copy.wait()
     for k in (1, 3, 2):
-        send(remote(chunk(mine), chunk(mine), kv1_ss.at[k], kv_rs.at[mine], first[k - 1]))
+        used = (core == 0) | y_targets[k - 1]
+        send(remote(chunk(mine), chunk(mine), kv1_ss.at[k], kv_rs.at[mine], first[k - 1]), used)
     own_rows = [qbuf.at[h, rows_at(z, HALF)] for h in range(2)]
     send(remote(swap, own_rows[1], swap_ss, q_rs.at[1, z], lines[1][0]))
     for k in (1, 7, 2, 6, 3, 5, 4):
         send(remote(own_rows[0], own_rows[0], q_ss.at[0, k], q_rs.at[0, z], lines[0][k]))
     for k in (1, 3, 2):
-        send(remote(chunk(mine), chunk(mine), kv2_ss.at[0, k], kv_rs.at[mine], second[k - 1]))
+        used = (core == 1) | y_targets[k - 1]
+        send(remote(chunk(mine), chunk(mine), kv2_ss.at[0, k], kv_rs.at[mine], second[k - 1]), used)
     remote(own_rows[1], own_rows[1], swap_ss, q_rs.at[1, z], partner).wait_recv()
     for k in (1, 7, 2, 6, 3, 5, 4):
         send(remote(own_rows[1], own_rows[1], q_ss.at[1, k], q_rs.at[1, z], lines[0][k]))
@@ -132,11 +145,14 @@
 
     lax.fori_loop(0, 2, clear, 0)
 
-    for j in (1, 3, 2):
-        n = jnp.where(core == 0, y * X + ring(x, -j, X), ring(y, -j, Y) * X + x)
-        remote(chunk(n), chunk(n), kv1_ss.at[j], kv_rs.at[n], partner).wait_recv()
+    for j, k in enumerate((1, 3, 2)):
+        source = jnp.where(jnp.int32(j) >= y, j + 1, j)
+        n = jnp.where(core == 0, y * X + ring(x, -k, X), source * X + x)
+        came = (core == 0) | needed(source, y)
+        when(came, remote(chunk(n), chunk(n), kv1_ss.at[j], kv_rs.at[n], partner).wait_recv)
         for k in (1, 3, 2):
-            send(remote(chunk(n), chunk(n), kv2_ss.at[j, k], kv_rs.at[n], second[k - 1]))
+            used = jnp.where(core == 0, y_targets[k - 1], came)
+            send(remote(chunk(n), chunk(n), kv2_ss.at[j + 1, k], kv_rs.at[n], second[k - 1]), used)
 
     def spread(parts):
         highest = jnp.max(functools.reduce(jnp.maximum, parts), axis=1, keepdims=True)
@@ -265,35 +281,32 @@
 
         lax.fori_loop(0, 4, one, 0)
 
-    def superblock(e):
-        return ring(y, jnp.where(e == 0, 0, jnp.where(e == 1, 3, e - 1)), Y)
-
-    def work(i, _):
-        early = i < 8
-        late = i - 8
-        e = jnp.where(early, lax.div(i, 4), 2 + lax.rem(i, 2))
-        j = jnp.where(early, 3 - lax.rem(i, 4), lax.div(late, 2))
-        h = 1 - lax.div(j, 2)
-        g = jnp.where(lax.rem(j, 2) == 0, 1 - near, near)
-        yp = superblock(e)
-
-        @pl.when((early & (lax.rem(i, 4) == 0)) | (i == 8) | (i == 9))
-        def _():
-            need_keys(yp)
-
-        @pl.when(i < 4)
-        def _():
-            need_queries(h, g)
-
-        task(h, g, yp)
-
-        @pl.when((i > 8) & (lax.rem(i, 2) == 1))
-        def _():
-            finish(h, g)
-
+    last = [jnp.maximum(y - 1, 0), ym]
+
+    def superblock(e, _):
+        yp = jnp.where(e == 0, y, jnp.where(e - 1 >= y, e, e - 1))
+        need_keys(yp)
+
+        def group(i, _):
+            h = jnp.where(lax.div(i, 2) == 0, jnp.where(y < ym, 0, 1), jnp.where(y < ym, 1, 0))
+            g = jnp.where(lax.rem(i, 2) == 0, 1 - near, near)
+
+            @pl.when(e == 0)
+            def _():
+                need_queries(h, g)
+
+            task(h, g, yp)
+
+            @pl.when(yp == jnp.where(h == 0, last[0], last[1]))
+            def _():
+                finish(h, g)
+
+            return 0
+
+        lax.fori_loop(0, 4, group, 0)
         return 0
 
-    lax.fori_loop(0, 16, work, 0)
+    lax.fori_loop(0, jnp.maximum(y, ym) + 1, superblock, 0)
 
     def merge(h, _):
         for s in range(Z):
@@ -316,8 +329,8 @@
     att_copy = remote(att.at[core], att.at[core], c_ss.at[1], c_rs.at[1], partner)
     att_copy.start()
 
-    for copy in sent:
-        copy.wait_send()
+    for condition, copy in sent:
+        when(condition, copy.wait_send)
 
     def drain(s, _):
         for h in range(2):
@@ -335,15 +348,9 @@
     att_copy.wait_send()
     remote(att.at[other], att.at[other], c_ss.at[1], c_rs.at[1], partner).wait_recv()
     both = jnp.concatenate([att[0], att[1]], axis=1)
-    outs = []
     for n in range(4):
         span = slice(n * 512, (n + 1) * 512)
-        proj[:, span] = jnp.dot(both, w2[:, span], preferred_element_type=F32).astype(BF16)
-        copy = pltpu.make_async_copy(proj.at[:, span], out_ref.at[:, span], out_s.at[n])
-        copy.start()
-        outs.append(copy)
-    for copy in outs:
-        copy.wait()
+        out_ref[:, span] = jnp.dot(both, w2[:, span], preferred_element_type=F32).astype(BF16)
 
 
 def per_device(queries, keys, values, out_weight):
@@ -351,9 +358,9 @@
     dma = pltpu.SemaphoreType.DMA
     return pl.pallas_call(
         attention_kernel,
-        out_shape=jax.ShapeDtypeStruct((ROWS, WIDTH), BF16),
+        out_shape=pltpu.VMEM((ROWS, WIDTH), BF16),
         in_specs=[hbm] * 4,
-        out_specs=hbm,
+        out_specs=pl.BlockSpec(memory_space=pltpu.VMEM),
         scratch_shapes=[
             pltpu.VMEM((2, LINE, HD), BF16),
             pltpu.VMEM((2, Y * SUPER, HD), BF16),

time: 65.6 us -> 62 us (0.945)
  the two profiles are of different devices: /device:TPU:1 before, /device:TPU:17 now
where the time goes in v4:
time: 62 us
  Pallas kernels  60.8 us (98%)
  local copies, waits for them, and re-layouts  1.15 us (2%)
    pallas_call x1, Pallas kernels, per_device(): pl.pallas_call(attention_kernel, out_shape=pltpu.VMEM((ROWS, WIDTH), BF16...  60.8 us

profile of v4, /device:TPU:17, one launch (start us, length us, event | category | flops | bytes accessed | tf_op | source)
XLA Modules:
  0.0 62.0 jit_solution(7521241430170604595)
XLA Ops:
  0.0 60.8 %shard_map.46 = bf16[384,2048]{1,0:T(8,128)(2,1)S(1)} custom-call(bf16[384,128]{1,0:T(8,128)(2,1)} %bitcast.5, bf16[384,128]{1,0:T(8,128)(2,1)} %bitcast.6, bf16[384,128]{1,0:T(8,128)(2,1)} %bitcast.7, bf16[128,4096]{1,0:T(8,128)(2,1)} %bitcast.4), custom_call_target="tpu_custom_call" | custom-call | tf_op jit(solution)/shard_map/pallas_call | solution.py:359
  60.8 1.1 %copy.6 = bf16[384,2048]{1,0:T(8,128)(2,1)} copy(bf16[384,2048]{1,0:T(8,128)(2,1)S(1)} %shard_map.46) | data formatting | bytes 3145728

commit v5 on v4

--- a/solution.py
+++ b/solution.py
@@ -49,8 +49,8 @@
 
 def attention_kernel(
     q_ref, k_ref, v_ref, w_ref, out_ref,
-    qbuf, kvbuf, kt, swap, acc, top, obuf, rbuf, att, w2, proj,
-    in_s, kv1_ss, kv2_ss, kv_rs, swap_ss, q_ss, q_rs, o_ss, o_rs, c_ss, c_rs, out_s,
+    qbuf, kvbuf, kt, swap, acc, top, obuf, rbuf, att, w2,
+    in_s, kv1_ss, kv2_ss, kv_rs, swap_ss, q_ss, q_rs, o_ss, o_rs, c_ss, c_rs,
 ):
     index, core = lax.axis_index("ctx"), lax.axis_index("head")
     x, z, y = lax.rem(index, X), lax.rem(lax.div(index, X), Z), lax.div(index, X * Z)
@@ -281,32 +281,48 @@
 
         lax.fori_loop(0, 4, one, 0)
 
-    last = [jnp.maximum(y - 1, 0), ym]
-
-    def superblock(e, _):
-        yp = jnp.where(e == 0, y, jnp.where(e - 1 >= y, e, e - 1))
-        need_keys(yp)
-
-        def group(i, _):
-            h = jnp.where(lax.div(i, 2) == 0, jnp.where(y < ym, 0, 1), jnp.where(y < ym, 1, 0))
-            g = jnp.where(lax.rem(i, 2) == 0, 1 - near, near)
-
-            @pl.when(e == 0)
-            def _():
-                need_queries(h, g)
-
-            task(h, g, yp)
-
-            @pl.when(yp == jnp.where(h == 0, last[0], last[1]))
-            def _():
-                finish(h, g)
-
+    count = jnp.maximum(y, ym) + 1
+
+    def superblock(e):
+        return jnp.where(e == 0, y, jnp.where(e - 1 >= y, e, e - 1))
+
+    def need_more(e, _):
+        need_keys(superblock(e))
+        return 0
+
+    def work(i, _):
+        early = i < 4
+        n = jnp.where(early, i, i - 4)
+        before = jnp.where(y < ym, 0, 1)
+        h = jnp.where(early, lax.rem(n, 2), jnp.where(lax.div(n, 2) == 0, before, 1 - before))
+        close = jnp.where(early, lax.div(n, 2) == 0, lax.rem(n, 2) == 1)
+        g = jnp.where(close, near, 1 - near)
+
+        @pl.when(i == 0)
+        def _():
+            need_keys(y)
+
+        @pl.when(early)
+        def _():
+            need_queries(h, g)
+
+        @pl.when(i == 4)
+        def _():
+            lax.fori_loop(1, count, need_more, 0)
+
+        def one(e, _):
+            task(h, g, superblock(e))
             return 0
 
-        lax.fori_loop(0, 4, group, 0)
+        lax.fori_loop(jnp.where(early, 0, 1), jnp.where(early, 1, count), one, 0)
+
+        @pl.when(early == ((y == 0) & (h == 0)))
+        def _():
+            finish(h, g)
+
         return 0
 
-    lax.fori_loop(0, jnp.maximum(y, ym) + 1, superblock, 0)
+    lax.fori_loop(0, 8, work, 0)
 
     def merge(h, _):
         for s in range(Z):
@@ -323,11 +339,14 @@
         for s in range(Z):
             merged = merged + rbuf[h, s, 0:HALF, :].astype(F32) * lane_columns(shares[s] / total)
         att[core, rows_at(h, HALF), :] = merged.astype(BF16)
+        att_copy(h, core).start()
         return 0
 
+    def att_copy(h, c):
+        rows = att.at[c, rows_at(h, HALF)]
+        return remote(rows, rows, c_ss.at[1 + h], c_rs.at[1 + h], partner)
+
     lax.fori_loop(0, 2, merge, 0)
-    att_copy = remote(att.at[core], att.at[core], c_ss.at[1], c_rs.at[1], partner)
-    att_copy.start()
 
     for condition, copy in sent:
         when(condition, copy.wait_send)
@@ -345,12 +364,15 @@
     loads[4].wait()
     w_other = w2.at[rows_at(other, HD)]
     remote(w_other, w_other, c_ss.at[0], c_rs.at[0], partner).wait_recv()
-    att_copy.wait_send()
-    remote(att.at[other], att.at[other], c_ss.at[1], c_rs.at[1], partner).wait_recv()
-    both = jnp.concatenate([att[0], att[1]], axis=1)
-    for n in range(4):
-        span = slice(n * 512, (n + 1) * 512)
-        out_ref[:, span] = jnp.dot(both, w2[:, span], preferred_element_type=F32).astype(BF16)
+    for h in range(2):
+        span = slice(h * HALF, (h + 1) * HALF)
+        att_copy(h, other).wait_recv()
+        both = jnp.concatenate([att[0, span, :], att[1, span, :]], axis=1)
+        for n in range(4):
+            columns = slice(n * 512, (n + 1) * 512)
+            out_ref[span, columns] = jnp.dot(both, w2[:, columns], preferred_element_type=F32).astype(BF16)
+    for h in range(2):
+        att_copy(h, core).wait_send()
 
 
 def per_device(queries, keys, values, out_weight):
@@ -372,9 +394,8 @@
             pltpu.VMEM((2, Z, MESSAGE, HD), BF16),
             pltpu.VMEM((2, ROWS, HD), BF16),
             pltpu.VMEM((2 * HD, WIDTH), BF16),
-            pltpu.VMEM((ROWS, WIDTH), BF16),
             dma((5,)), dma((4,)), dma((4, 4)), dma((16,)), dma, dma((2, 8)), dma((2, 8)), dma((2, 8)), dma((2, 8)),
-            dma((2,)), dma((2,)), dma((4,)),
+            dma((3,)), dma((3,)),
         ],
         compiler_params=pltpu.CompilerParams(
             collective_id=0, has_side_effects=True, vmem_limit_bytes=56 << 20

time: 62 us -> 60.1 us (0.969)
  the two profiles are of different devices: /device:TPU:17 before, /device:TPU:24 now
where the time goes in v5:
time: 60.1 us; the launch traced here: 59.5 us
  Pallas kernels  58.3 us (97%)
  local copies, waits for them, and re-layouts  1.15 us (2%)
    pallas_call x1, Pallas kernels, per_device(): pl.pallas_call(attention_kernel, out_shape=pltpu.VMEM((ROWS, WIDTH), BF16...  58.3 us

profile of v5, /device:TPU:24, one launch (start us, length us, event | category | flops | bytes accessed | tf_op | source)
XLA Modules:
  0.0 59.5 jit_solution(10856461085512364801)
XLA Ops:
  0.0 58.3 %shard_map.46 = bf16[384,2048]{1,0:T(8,128)(2,1)S(1)} custom-call(bf16[384,128]{1,0:T(8,128)(2,1)} %bitcast.5, bf16[384,128]{1,0:T(8,128)(2,1)} %bitcast.6, bf16[384,128]{1,0:T(8,128)(2,1)} %bitcast.7, bf16[128,4096]{1,0:T(8,128)(2,1)} %bitcast.4), custom_call_target="tpu_custom_call" | custom-call | tf_op jit(solution)/shard_map/pallas_call | solution.py:381
  58.3 1.1 %copy.6 = bf16[384,2048]{1,0:T(8,128)(2,1)} copy(bf16[384,2048]{1,0:T(8,128)(2,1)S(1)} %shard_map.46) | data formatting | bytes 3145728

commit v6 on v5

--- a/solution.py
+++ b/solution.py
@@ -126,12 +126,12 @@
     send(remote(swap, own_rows[1], swap_ss, q_rs.at[1, z], lines[1][0]))
     for k in (1, 7, 2, 6, 3, 5, 4):
         send(remote(own_rows[0], own_rows[0], q_ss.at[0, k], q_rs.at[0, z], lines[0][k]))
+    remote(own_rows[1], own_rows[1], swap_ss, q_rs.at[1, z], partner).wait_recv()
+    for k in (1, 7, 2, 6, 3, 5, 4):
+        send(remote(own_rows[1], own_rows[1], q_ss.at[1, k], q_rs.at[1, z], lines[0][k]))
     for k in (1, 3, 2):
         used = (core == 1) | y_targets[k - 1]
         send(remote(chunk(mine), chunk(mine), kv2_ss.at[0, k], kv_rs.at[mine], second[k - 1]), used)
-    remote(own_rows[1], own_rows[1], swap_ss, q_rs.at[1, z], partner).wait_recv()
-    for k in (1, 7, 2, 6, 3, 5, 4):
-        send(remote(own_rows[1], own_rows[1], q_ss.at[1, k], q_rs.at[1, z], lines[0][k]))
     send(
         remote(
             w_ref.at[:, rows_at(other, WIDTH)], w2.at[rows_at(core, HD)], c_ss.at[0], c_rs.at[0], partner
@@ -286,10 +286,6 @@
     def superblock(e):
         return jnp.where(e == 0, y, jnp.where(e - 1 >= y, e, e - 1))
 
-    def need_more(e, _):
-        need_keys(superblock(e))
-        return 0
-
     def work(i, _):
         early = i < 4
         n = jnp.where(early, i, i - 4)
@@ -306,11 +302,11 @@
         def _():
             need_queries(h, g)
 
-        @pl.when(i == 4)
-        def _():
-            lax.fori_loop(1, count, need_more, 0)
-
         def one(e, _):
+            @pl.when(i == 4)
+            def _():
+                need_keys(superblock(e))
+
             task(h, g, superblock(e))
             return 0
 

time: 60.1 us -> 59.6 us (level)
  no operation moved by 1% of the time
where the time goes in v6:
time: 59.6 us; the launch traced here: 59.5 us
  Pallas kernels  58.4 us (98%)
  local copies, waits for them, and re-layouts  1.15 us (2%)
    pallas_call x1, Pallas kernels, per_device(): pl.pallas_call(attention_kernel, out_shape=pltpu.VMEM((ROWS, WIDTH), BF16...  58.4 us

profile of v6, /device:TPU:24, one launch (start us, length us, event | category | flops | bytes accessed | tf_op | source)
XLA Modules:
  0.0 59.5 jit_solution(621968579513017939)
XLA Ops:
  0.0 58.4 %shard_map.46 = bf16[384,2048]{1,0:T(8,128)(2,1)S(1)} custom-call(bf16[384,128]{1,0:T(8,128)(2,1)} %bitcast.5, bf16[384,128]{1,0:T(8,128)(2,1)} %bitcast.6, bf16[384,128]{1,0:T(8,128)(2,1)} %bitcast.7, bf16[128,4096]{1,0:T(8,128)(2,1)} %bitcast.4), custom_call_target="tpu_custom_call" | custom-call | tf_op jit(solution)/shard_map/pallas_call | solution.py:377
  58.4 1.1 %copy.6 = bf16[384,2048]{1,0:T(8,128)(2,1)} copy(bf16[384,2048]{1,0:T(8,128)(2,1)S(1)} %shard_map.46) | data formatting | bytes 3145728

commit v7 on v6

--- a/solution.py
+++ b/solution.py
@@ -17,6 +17,7 @@
 SUPER = X * ROWS
 TILE = LINE // 2
 BLOCK = 512
+PART = 256
 WIDTH = 2048
 MESSAGE = HALF + 16
 SCALE2 = math.log2(math.e) / math.sqrt(HD)
@@ -174,7 +175,7 @@
         return jnp.concatenate([values, jnp.ones(values.shape, BF16)], axis=1)
 
     def attend(h, g, yp):
-        spans = [pl.ds(pl.multiple_of(g * TILE + t * ROWS, ROWS), ROWS) for t in range(TILE // ROWS)]
+        spans = [pl.ds(pl.multiple_of(g * TILE + t * PART, PART), PART) for t in range(TILE // PART)]
 
         def scores(span):
             return [piece for b in range(SUPER // BLOCK) for piece in score(h, span, yp, b)]

time: 59.6 us -> 60.1 us (level)
  no operation moved by 1% of the time
where the time goes in v7:
time: 60.1 us
  Pallas kernels  58.9 us (98%)
  local copies, waits for them, and re-layouts  1.15 us (2%)
    pallas_call x1, Pallas kernels, per_device(): pl.pallas_call(attention_kernel, out_shape=pltpu.VMEM((ROWS, WIDTH), BF16...  58.9 us

profile of v7, /device:TPU:24, one launch (start us, length us, event | category | flops | bytes accessed | tf_op | source)
XLA Modules:
  0.0 60.1 jit_solution(13111967036975497425)
XLA Ops:
  0.0 58.9 %shard_map.46 = bf16[384,2048]{1,0:T(8,128)(2,1)S(1)} custom-call(bf16[384,128]{1,0:T(8,128)(2,1)} %bitcast.5, bf16[384,128]{1,0:T(8,128)(2,1)} %bitcast.6, bf16[384,128]{1,0:T(8,128)(2,1)} %bitcast.7, bf16[128,4096]{1,0:T(8,128)(2,1)} %bitcast.4), custom_call_target="tpu_custom_call" | custom-call | tf_op jit(solution)/shard_map/pallas_call | solution.py:378
  58.9 1.1 %copy.6 = bf16[384,2048]{1,0:T(8,128)(2,1)} copy(bf16[384,2048]{1,0:T(8,128)(2,1)S(1)} %shard_map.46) | data formatting | bytes 3145728
